TPU v7x, 32 devices: a whole 2x2x4 slice. The times are simulated.
32 devices in a mesh: grp: 2 (over x), aux: 16 (over z, y, core).
Axes of the slice: x: 2, y: 2, z: 4, core: 2. Of those that a mesh axis runs over, the one named last changes fastest.
Arguments:
- three_index: bfloat16 [128, 256, 256], P('grp', 'aux'), parts along dimension 0, may hold values from -6 to 6
- fit_metric: float32 [512, 16], P(('grp', 'aux')), parts along dimension 0, as said below
- fit_blocks: int32 [128, 12], P('grp'), parts along dimension 0, may hold values from 0 to 15, as said below
- domains: int32 [128, 256], P('grp'), parts along dimension 0, may hold values from 0 to 19999
- occ_energy: float32 [128], P('grp'), parts along dimension 0, may hold values from -1.5 to -0.3
- virt_energy: float32 [40000], P('grp'), parts along dimension 0, may hold values from 0.2 to 3
- owner_map: int32 [128], P('grp'), parts along dimension 0, may hold values from 0 to 63, as said below
- partners: int32 [32, 8], P('grp'), parts along dimension 0, may hold values from 0 to 63, as said below
Outputs:
- slab_energy: float32 [128, 4], P(('grp', 'aux')), parts along dimension 0
- partner_energy: float32 [128, 8], P(('grp', 'aux')), parts along dimension 0
- energy_per_orbital: float32 [2], P('grp'), parts along dimension 0
There are 2 independent parts, one for each index of `grp`. A program takes and returns all parts, laid end to end along the dimension named above; each array names one. Nothing has to cross between parts.
Inputs may be any that keep to these rules, and one draw needn't show every extreme that they name: `owner_map`: A permutation of the occupied orbitals. `partners`: each row lists 8 different orbitals, none of them held by that slab. `fit_blocks`: each row lists 12 different auxiliary blocks. `fit_metric`: each block of 16 consecutive rows holds that block's weights.
All inputs are finite; a program needn't handle non-finite values.
Results may differ from a plain program's by a relative error of at most 0.0003.
Values may be sent and summed in bfloat16 or wider, within the bound.
A program may use at most 128 MiB of HBM per device.

v0:
```python
import jax
import jax.numpy as jnp
from jax import lax
from jax.sharding import PartitionSpec as P


def pair_energy(left, right, left_ids, right_ids, row_mask, domains, occ_energy, virt_energy):
    masked = left * row_mask[:, :, None]
    coulomb = jnp.einsum("ipa,jpb->ijab", masked, right, preferred_element_type=jnp.float32)
    left_gap = jnp.take(virt_energy, domains[left_ids], axis=0) - occ_energy[left_ids][:, None]
    right_gap = jnp.take(virt_energy, domains[right_ids], axis=0) - occ_energy[right_ids][:, None]
    divisor = left_gap[:, None, :, None] + right_gap[None, :, None, :]
    return -jnp.sum(coulomb * coulomb / divisor, axis=(2, 3))


def per_device(
    three_index, fit_metric, fit_blocks, domains, occ_energy, virt_energy, owner_map, partners
):
    n_devices = lax.axis_size("aux")
    my_index = lax.axis_index("aux")
    total_occ, block_rows, dom_width = three_index.shape
    slab_size = total_occ // n_devices
    fitted = jnp.einsum(
        "pq,iqa->ipa", fit_metric, three_index.astype(jnp.float32), precision=lax.Precision.HIGHEST
    ).astype(jnp.bfloat16)
    slab_table = owner_map.reshape(n_devices, slab_size)
    own_ids = lax.dynamic_index_in_dim(slab_table, my_index, 0, keepdims=False)
    part_ids = lax.dynamic_index_in_dim(partners, my_index, 0, keepdims=False)
    listed = fit_blocks[own_ids]
    hits = jnp.any(
        listed[:, :, None] == jnp.arange(n_devices, dtype=jnp.int32)[None, None, :], axis=1
    )
    row_mask = jnp.repeat(hits.astype(jnp.bfloat16), block_rows, axis=1)
    joined = jnp.concatenate([slab_table, partners], axis=1)
    arrived = lax.all_to_all(fitted[joined.T], "aux", split_axis=1, concat_axis=1, tiled=True)
    arrived_all = arrived.reshape(arrived.shape[0], n_devices * block_rows, dom_width)
    own = arrived_all[:slab_size]
    mates = arrived_all[slab_size:]
    slab_energy = pair_energy(
        own, own, own_ids, own_ids, row_mask, domains, occ_energy, virt_energy
    )
    partner_energy = pair_energy(
        own, mates, own_ids, part_ids, row_mask, domains, occ_energy, virt_energy
    )
    local_total = jnp.sum(slab_energy) + jnp.sum(partner_energy)
    whole_total = lax.psum(local_total, "aux")
    return (slab_energy, partner_energy, (whole_total / total_occ).reshape(1))


def solution(mesh):
    in_specs = (
        P("grp", "aux", None),
        P(("grp", "aux"), None),
        P("grp", None),
        P("grp", None),
        P("grp"),
        P("grp"),
        P("grp"),
        P("grp", None),
    )
    out_specs = (P(("grp", "aux"), None), P(("grp", "aux"), None), P("grp"))
    return jax.shard_map(
        per_device, mesh=mesh, in_specs=in_specs, out_specs=out_specs, check_vma=False
    )
```

profile of v0, /device:TPU:0, one launch (start us, length us, event | category | flops | bytes accessed | tf_op | source)
XLA Modules:
  0.0 92.6 jit_solution(9493693099025295637)
XLA Ops:
  0.6 0.0 copy-start
  0.6 0.8 reshape.128
  1.4 0.1 copy.22
  1.5 0.7 compare_select_fusion.2
  2.2 0.1 reshape.140
  2.3 0.0 copy-done
  2.3 1.3 %fusion = bf16[64,16,256]{2,1,0:T(8,128)(2,1)S(1)} fusion(bf16[64,16,256]{2,1,0:T(8,128)(2,1)S(1)} %copy-done, f32[16,16]{1,0:T(8,128)} %param.11), kind=kOutput, calls=%fused_computation.13 | convolution fusion | flops 50593792 | bytes 1049600 | tf_op jit(solution)/shard_map/pq,iqa->ipa/dot_general | solution.py:23
  3.6 0.8 gather_fusion
  4.4 1.3 %copy.23 = bf16[12,16,16,256]{3,2,0,1:T(8,128)(2,1)} copy(bf16[12,16,16,256]{3,2,1,0:T(8,128)(2,1)S(1)} %bitcast.66) | data formatting | bytes 3145728 | tf_op jit(solution)/shard_map/gather | solution.py:35
  5.7 0.0 copy-start.4
  5.7 0.0 copy-start.3
  5.7 0.0 copy-start.1
  5.7 0.0 copy-start.2
  5.7 7.5 %all-to-all-start = ((bf16[12,16,16,256]{3,2,0,1:T(8,128)(2,1)}), bf16[12,16,16,256]{3,2,0,1:T(8,128)(2,1)S(1)}, u32[]{:S(2)}, u32[]{:S(2)}) async-start(bf16[12,16,16,256]{3,2,0,1:T(8,128)(2,1)} %copy.23), calls=%async_computation | async-start | bytes 3145728 | tf_op jit(solution)/shard_map/all_to_all | solution.py:35
  13.3 0.0 copy-done.4
  13.3 0.2 dynamic-slice_reduce_fusion
  13.5 0.0 copy-done.3
  13.5 0.6 gather_fusion.2
  14.1 0.0 copy-done.1
  14.1 0.6 gather_fusion.3
  14.7 0.6 gather_fusion.4
  15.3 0.6 gather_fusion.6
  16.0 0.0 copy-done.2
  16.0 0.0 copy-start.5
  16.0 6.2 %gather_fusion.7 = f32[1024]{0:T(1024)S(1)} fusion(f32[20000]{0:T(1024)S(1)} %copy-done.2, s32[1024]{0:T(1024)S(1)} %broadcast_clamp_fusion.1), kind=kCustom, calls=%fused_computation.clone | custom fusion | bytes 12288 | tf_op jit(solution)/shard_map/jit(_take)/gather | solution.py:10
  22.2 0.0 copy-done.5
  22.2 0.1 copy.25
  22.3 0.6 gather_fusion.1
  22.8 0.1 copy.26
  22.9 0.1 fusion.10
  23.1 11.8 %gather_fusion.5 = f32[2048]{0:T(1024)S(1)} fusion(f32[20000]{0:T(1024)S(1)} %copy-done.2, s32[2048]{0:T(1024)S(1)} %broadcast_clamp_fusion), kind=kCustom, calls=%fused_computation.6 | custom fusion | bytes 24576 | tf_op jit(solution)/shard_map/jit(_take)/gather | solution.py:11
  34.9 0.1 select_subtract_fusion.1
  35.0 0.1 select_subtract_fusion
  35.0 10.2 %all-to-all-done = bf16[12,16,16,256]{3,2,0,1:T(8,128)(2,1)S(1)} async-done(((bf16[12,16,16,256]{3,2,0,1:T(8,128)(2,1)}), bf16[12,16,16,256]{3,2,0,1:T(8,128)(2,1)S(1)}, u32[]{:S(2)}, u32[]{:S(2)}) %all-to-all-start) | async-done | bytes 1572896 | tf_op jit(solution)/shard_map/all_to_all | solution.py:35
  45.3 2.0 %fusion.17 = (f32[]{:T(128)}, f32[4,4]{0,1:T(4,128)S(1)}) fusion(f32[4,256]{1,0:T(4,128)S(1)} %select_subtract_fusion.1, bf16[4,16]{1,0:T(4,128)(2,1)S(1)} %convert_element_type.12, bf16[12,16,16,256]{3,2,0,1:T(8,128)(2,1)S(1)} %all-to-all-done), kind=kOutput, calls=%fused_computation.47 | convolution fusion | flops 543162368 | bytes 1057860 | tf_op jit(solution)/shard_map/ipa,jpb->ijab/dot_general | solution.py:9
  47.2 0.7 copy.28
  47.9 3.4 %fusion.16 = (f32[]{:T(128)}, f32[4,8]{0,1:T(8,128)S(1)}) fusion(f32[8,256]{1,0:T(8,128)S(1)} %select_subtract_fusion, f32[4,256]{1,0:T(4,128)S(1)} %select_subtract_fusion.1, bf16[4,16]{1,0:T(4,128)(2,1)S(1)} %convert_element_type.12, bf16[12,16,16,256]{3,2,0,1:T(8,128)(2,1)S(1)} %all-to-all-done), kind=kOutput, calls=%fused_computation.46 | convolution fusion | flops 1085276160 | bytes 1585412 | tf_op jit(solution)/shard_map/ipa,jpb->ijab/dot_general | solution.py:9
  52.6 0.7 copy.29
  53.2 37.6 %psum.7 = f32[]{:T(128)} all-reduce(f32[]{:T(128)S(6)} %add.116), channel_id=1, replica_groups=mesh['grp'=2,'aux'=16] {'aux'}, use_global_device_ids=true, to_apply=%region_5.7 | all-reduce | flops 1 | bytes 8 | tf_op jit(solution)/shard_map/psum | solution.py:46
  (16 shorter events, 0.1 us)
Async XLA Ops:
  0.6 1.7 %copy-start = (bf16[64,16,256]{2,1,0:T(8,128)(2,1)S(1)}, bf16[64,16,256]{2,1,0:T(8,128)(2,1)}, u32[]{:S(2)}) copy-start(bf16[64,16,256]{2,1,0:T(8,128)(2,1)} %param.10) | copy-start | bytes 1572868
  5.7 7.6 %copy-start.4 = (s32[16,8]{0,1:T(8,128)S(1)}, s32[16,8]{0,1:T(8,128)}, u32[]{:S(2)}) copy-start(s32[16,8]{0,1:T(8,128)} %param.17) | copy-start | bytes 1540
  5.7 7.8 %copy-start.3 = (s32[64,256]{1,0:T(8,128)S(1)}, s32[64,256]{1,0:T(8,128)}, u32[]{:S(2)}) copy-start(s32[64,256]{1,0:T(8,128)} %param.13) | copy-start | bytes 196612
  5.7 8.3 %copy-start.1 = (f32[64]{0:T(128)S(1)}, f32[64]{0:T(128)}, u32[]{:S(2)}) copy-start(f32[64]{0:T(128)} %param.14) | copy-start | bytes 772
  5.7 10.2 %copy-start.2 = (f32[20000]{0:T(1024)S(1)}, f32[20000]{0:T(1024)}, u32[]{:S(2)}) copy-start(f32[20000]{0:T(1024)} %param.15) | copy-start | bytes 240004
  5.7 39.5 %all-to-all-start = ((bf16[12,16,16,256]{3,2,0,1:T(8,128)(2,1)}), bf16[12,16,16,256]{3,2,0,1:T(8,128)(2,1)S(1)}, u32[]{:S(2)}, u32[]{:S(2)}) async-start(bf16[12,16,16,256]{3,2,0,1:T(8,128)(2,1)} %copy.23), calls=%async_computation | async-start | bytes 3145728 | tf_op jit(solution)/shard_map/all_to_all | solution.py:35
  16.0 6.2 %copy-start.5 = (s32[64,12]{0,1:T(8,128)S(1)}, s32[64,12]{0,1:T(8,128)}, u32[]{:S(2)}) copy-start(s32[64,12]{0,1:T(8,128)} %param.12) | copy-start | bytes 9220
where the time goes:
time: 93 us; the launch traced here: 92.6 us
  blocking collectives  37.6 us (40%)
  local copies, waits for them, and re-layouts  25.7 us (28%)
  waiting for transfers between devices  10.2 us (11%)
  starting transfers between devices  7.53 us (8%)
  matrix products  6.6 us (7%)
  between operations  3.9 us (4%)
  other arithmetic  1 us (1%)
    psum x1, blocking collectives, per_device(): whole_total = lax.psum(local_total, 'aux')  37.6 us
    gather x2, local copies, waits for them, and re-layouts, pair_energy(): jnp.take(virt_energy, domains[right_ids], axis=0)  11.8 us
    all_to_all x1, waiting for transfers between devices, per_device(): lax.all_to_all(fitted[joined.T], 'aux', split_axis=1, concat_axis=1, tile...  10.2 us
    all_to_all x1, starting transfers between devices, per_device(): lax.all_to_all(fitted[joined.T], 'aux', split_axis=1, concat_axis=1, tile...  7.53 us
    gather x2, local copies, waits for them, and re-layouts, pair_energy(): jnp.take(virt_energy, domains[left_ids], axis=0)  6.16 us
    dot_general x2, matrix products, pair_energy(): jnp.einsum('ipa,jpb->ijab', masked, right, preferred_element_type=jnp.flo...  5.34 us
    gather x2, local copies, waits for them, and re-layouts, per_device(): fitted[joined.T]  2.14 us
  transfers between devices with their start and end apart: 1, of which 1 were waited for; matrix products, arithmetic and copies ran while one was open for 23% of the time, Pallas kernels for 0%

commit v1 on v0

v1 whole, which is shorter than its diff:
```python
import functools

import jax
import jax.numpy as jnp
from jax import lax
from jax.experimental import pallas as pl
from jax.experimental.pallas import tpu as pltpu
from jax.sharding import PartitionSpec as P

HIGHEST = lax.Precision.HIGHEST
LANES = 128


def kernel(
    n, slab, npart,
    owner_ref, partners_ref, blocks_ref, occ_ref,
    three_ref, metric_ref, domains_ref, table_ref,
    out_ref,
    fitted, send, recv, inverse, left_t, gaps, sums, totals,
    send_sem, recv_sem, tot_send_sem, tot_recv_sem,
):
    me = lax.axis_index("aux")
    total_occ, rows, width = three_ref.shape
    width_p = n * rows
    joined = slab + npart
    order_start = max(n // 2 - 1, 0)

    def peer(step):
        return lax.rem(me + 1 + lax.rem(step + order_start, n - 1), n)

    def orbital(t, slot):
        return owner_ref[t * slab + slot] if slot < slab else partners_ref[t, slot - slab]

    barrier = pltpu.get_barrier_semaphore()

    def greet(step, carry):
        pl.semaphore_signal(
            barrier, inc=1, device_id={"aux": peer(step)}, device_id_type=pl.DeviceIdType.MESH
        )
        return carry

    lax.fori_loop(0, n - 1, greet, 0)

    group = 256 // rows
    side = group * rows
    tall = jnp.concatenate([metric_ref[...]] * group, axis=0)
    spread = (
        lax.broadcasted_iota(jnp.int32, (rows, side), 1) % rows
        == lax.broadcasted_iota(jnp.int32, (rows, side), 0)
    ).astype(jnp.float32)
    tiled = jnp.dot(tall, spread, precision=HIGHEST, preferred_element_type=jnp.float32)
    same = (
        lax.broadcasted_iota(jnp.int32, (side, side), 0) // rows
        == lax.broadcasted_iota(jnp.int32, (side, side), 1) // rows
    )
    weights = jnp.where(same, tiled, 0.0)
    first = weights.astype(jnp.bfloat16)
    rest = weights - first.astype(jnp.float32)
    second = rest.astype(jnp.bfloat16)
    third = (rest - second.astype(jnp.float32)).astype(jnp.bfloat16)

    def fit(g, carry):
        block = three_ref[pl.ds(g * group, group)].reshape(side, width)
        done = jnp.dot(third, block, preferred_element_type=jnp.float32)
        done += jnp.dot(second, block, preferred_element_type=jnp.float32)
        done += jnp.dot(first, block, preferred_element_type=jnp.float32)
        fitted[pl.ds(g * group, group)] = done.astype(jnp.bfloat16).reshape(group, rows, width)
        return carry

    lax.fori_loop(0, total_occ // group, fit, 0)

    pl.semaphore_wait(barrier, n - 1)

    def block_copy(target, source):
        return pltpu.make_async_remote_copy(
            src_ref=send.at[target], dst_ref=recv.at[source],
            send_sem=send_sem.at[target], recv_sem=recv_sem.at[source],
            device_id={"aux": target}, device_id_type=pl.DeviceIdType.MESH,
        )

    def pack(step, carry):
        t = peer(step)
        for slot in range(joined):
            send[t, slot] = fitted[orbital(t, slot)]
        block_copy(t, me).start()
        return carry

    lax.fori_loop(0, n - 1, pack, 0)
    for slot in range(joined):
        recv[me, slot] = fitted[orbital(me, slot)]

    depth = table_ref.shape[0]
    by_lane = table_ref[...].T
    for slot in range(joined):
        one = orbital(me, slot)
        index = domains_ref[pl.ds(one, 1), :]
        high = index // LANES
        low = index - high * LANES
        pick = (lax.broadcasted_iota(jnp.int32, (depth, width), 0) == high).astype(jnp.float32)
        values = jnp.dot(by_lane, pick, precision=HIGHEST, preferred_element_type=jnp.float32)
        chosen = jnp.where(lax.broadcasted_iota(jnp.int32, (LANES, width), 0) == low, values, 0.0)
        gaps[pl.ds(slot, 1), :] = jnp.sum(chosen, axis=0, keepdims=True) - occ_ref[one]
    for i in range(slab):
        down = jnp.broadcast_to(gaps[pl.ds(i, 1), :], (width, width)).T

        def invert(j, carry, i=i, down=down):
            inverse[i, j] = 1.0 / (down + gaps[pl.ds(j, 1), :])
            return carry

        lax.fori_loop(0, joined, invert, 0)
    sums[...] = jnp.zeros_like(sums)

    def arrive(step, carry):
        source = peer(step)
        block_copy(source, source).wait_recv()
        return carry

    lax.fori_loop(0, n - 1, arrive, 0)

    block_of = lax.broadcasted_iota(jnp.int32, (1, width_p), 1) // rows
    for i in range(slab):
        one = orbital(me, i)

        def hit(f, found, one=one):
            return jnp.where(block_of == blocks_ref[one, f], 1.0, found)

        mask = lax.fori_loop(
            0, blocks_ref.shape[1], hit, jnp.zeros((1, width_p), jnp.float32), unroll=width_p <= 512
        )
        turned = recv[:, i].reshape(width_p, width).astype(jnp.float32).T
        left_t[i] = (turned * mask).astype(jnp.bfloat16)

    def pairs(i, carry):
        left = left_t[i]
        for j in range(joined):
            right = recv[:, j].reshape(width_p, width)
            coulomb = jnp.dot(left, right, preferred_element_type=jnp.float32)
            terms = coulomb * coulomb * inverse[i, j]
            sums[i, pl.ds(j, 1), :] = jnp.sum(terms, axis=0, keepdims=True)
        return carry

    lax.fori_loop(0, slab, pairs, 0)

    ones = jnp.ones((8, width), jnp.float32)
    energies = [
        -lax.dot_general(
            ones, sums[i], (((1,), (1,)), ((), ())),
            precision=HIGHEST, preferred_element_type=jnp.float32,
        )[0:1]
        for i in range(slab)
    ]
    pad = jnp.zeros((8 - slab, LANES), jnp.float32)
    table = jnp.concatenate(energies + [pad], axis=0)
    totals[me] = table

    def total_copy(target, source):
        return pltpu.make_async_remote_copy(
            src_ref=totals.at[me], dst_ref=totals.at[source],
            send_sem=tot_send_sem.at[target], recv_sem=tot_recv_sem.at[source],
            device_id={"aux": target}, device_id_type=pl.DeviceIdType.MESH,
        )

    def give(step, carry):
        total_copy(peer(step), me).start()
        return carry

    lax.fori_loop(0, n - 1, give, 0)

    def take(step, carry):
        source = peer(step)
        total_copy(source, source).wait_recv()
        return carry

    lax.fori_loop(0, n - 1, take, 0)
    whole = jnp.sum(jnp.sum(totals[...], axis=0), axis=(0, 1), keepdims=True) / total_occ
    last = lax.broadcasted_iota(jnp.int32, (8, LANES), 0) == slab
    out_ref[...] = jnp.where(last, whole, table)

    def finish(step, carry):
        t = peer(step)
        block_copy(t, me).wait_send()
        total_copy(t, me).wait_send()
        return carry

    lax.fori_loop(0, n - 1, finish, 0)


def per_device(
    three_index, fit_metric, fit_blocks, domains, occ_energy, virt_energy, owner_map, partners
):
    n = lax.axis_size("aux")
    total_occ, rows, width = three_index.shape
    slab = total_occ // n
    npart = partners.shape[1]
    joined = slab + npart
    chunk = 8 * LANES
    length = -(-virt_energy.shape[0] // chunk) * chunk
    table = jnp.pad(virt_energy, (0, length - virt_energy.shape[0])).reshape(-1, LANES)
    smem = pl.BlockSpec(memory_space=pltpu.SMEM)
    vmem = pl.BlockSpec(memory_space=pltpu.VMEM)
    out = pl.pallas_call(
        functools.partial(kernel, n, slab, npart),
        out_shape=jax.ShapeDtypeStruct((8, LANES), jnp.float32),
        in_specs=[smem] * 4 + [vmem] * 4,
        out_specs=vmem,
        scratch_shapes=[
            pltpu.VMEM((total_occ, rows, width), jnp.bfloat16),
            pltpu.VMEM((n, joined, rows, width), jnp.bfloat16),
            pltpu.VMEM((n, joined, rows, width), jnp.bfloat16),
            pltpu.VMEM((slab, joined, width, width), jnp.float32),
            pltpu.VMEM((slab, width, n * rows), jnp.bfloat16),
            pltpu.VMEM((-(-joined // 8) * 8, width), jnp.float32),
            pltpu.VMEM((slab, LANES, width), jnp.float32),
            pltpu.VMEM((n, 8, LANES), jnp.float32),
            pltpu.SemaphoreType.DMA((n,)),
            pltpu.SemaphoreType.DMA((n,)),
            pltpu.SemaphoreType.DMA((n,)),
            pltpu.SemaphoreType.DMA((n,)),
        ],
        compiler_params=pltpu.CompilerParams(
            collective_id=0, has_side_effects=True, vmem_limit_bytes=56 * 1024 * 1024
        ),
    )(owner_map, partners, fit_blocks, occ_energy, three_index, fit_metric, domains, table)
    return out[:slab, :slab], out[:slab, slab:joined], out[slab, :1]


def solution(mesh):
    in_specs = (
        P("grp", "aux", None),
        P(("grp", "aux"), None),
        P("grp", None),
        P("grp", None),
        P("grp"),
        P("grp"),
        P("grp"),
        P("grp", None),
    )
    out_specs = (P(("grp", "aux"), None), P(("grp", "aux"), None), P("grp"))
    return jax.shard_map(
        per_device, mesh=mesh, in_specs=in_specs, out_specs=out_specs, check_vma=False
    )
```

time: 93 us -> 59.7 us (0.64)
  Pallas kernels: 0 us -> 52 us
  blocking collectives: 37.6 us -> 0 us
  local copies, waits for them, and re-layouts: 25.7 us -> 6.72 us
  waiting for transfers between devices: 10.2 us -> 0 us
  starting transfers between devices: 7.53 us -> 0 us
  matrix products: 6.6 us -> 0 us
  between operations: 3.9 us -> 0.66 us
  other arithmetic: 1 us -> 0 us
    pallas_call x0 -> x1, Pallas kernels: none -> 52 us  [per_device(): pl.pallas_call(functools.partial(kernel, n, slab, npart), out_shape=jax.S...]
    psum x1 -> x0, blocking collectives: 37.6 us -> none  [per_device(): whole_total = lax.psum(local_total, 'aux')]
    gather x12 -> x0, local copies, waits for them, and re-layouts: 23.2 us -> none  [the longest x2 11.8 us: pair_energy(): jnp.take(virt_energy, domains[right_ids], axis=0)]
    all_to_all x1 -> x0, waiting for transfers between devices: 10.2 us -> none  [per_device(): lax.all_to_all(fitted[joined.T], 'aux', split_axis=1, concat_axis=1, tile...]
    all_to_all x1 -> x0, starting transfers between devices: 7.53 us -> none  [per_device(): lax.all_to_all(fitted[joined.T], 'aux', split_axis=1, concat_axis=1, tile...]
    dot_general x3 -> x0, matrix products: 6.6 us -> none  [the longest x2 5.34 us: pair_energy(): jnp.einsum('ipa,jpb->ijab', masked, right, preferred_element_type=jnp.flo...]
    slice x0 -> x3, local copies, waits for them, and re-layouts: none -> 3.14 us  [per_device(): return (out[:slab, :slab], out[:slab, slab:joined], out[slab, :1])]
    unnamed x17 -> x6, local copies, waits for them, and re-layouts: 1.45 us -> 2.07 us
  transfers between devices with their start and end apart: 1 -> 0, of which waited for: 1 -> 0; matrix products, arithmetic and copies ran while one was open for 23% -> 0% of each run, Pallas kernels for 0% -> 0%
where the time goes in v1:
time: 59.7 us; the launch traced here: 59.3 us
  Pallas kernels  52 us (87%)
  local copies, waits for them, and re-layouts  6.72 us (11%)
  between operations  0.66 us (1%)
    pallas_call x1, Pallas kernels, per_device(): pl.pallas_call(functools.partial(kernel, n, slab, npart), out_shape=jax.S...  52 us
    slice x3, local copies, waits for them, and re-layouts, per_device(): return (out[:slab, :slab], out[:slab, slab:joined], out[slab, :1])  3.14 us
    unnamed x6, local copies, waits for them, and re-layouts  2.07 us
    reshape x1, local copies, waits for them, and re-layouts, per_device(): jnp.pad(virt_energy, (0, length - virt_energy.shape[0])).reshape(-1, LANES)  1.51 us

profile of v1, /device:TPU:0, one launch (start us, length us, event | category | flops | bytes accessed | tf_op | source)
XLA Modules:
  0.0 59.3 jit_solution(4469760263369023163)
XLA Ops:
  0.6 0.0 copy-start.1
  0.6 1.4 %copy.11.partners_ref = s32[16,8]{1,0:T(8,128)} copy(s32[16,8]{0,1:T(8,128)} %param.15) | data formatting | bytes 1024 | tf_op args[7]
  2.0 0.0 copy-done.1
  2.0 0.7 %copy.12.blocks_ref = s32[64,12]{1,0:T(8,128)} copy(s32[64,12]{0,1:T(8,128)S(1)} %copy-done.1) | data formatting | bytes 6144 | tf_op args[2]
  2.7 1.5 %pad_bitcast_fusion.table_ref = f32[160,128]{1,0:T(8,128)} fusion(f32[20000]{0:T(1024)} %param.13), kind=kLoop, calls=%fused_computation | loop fusion | bytes 161920 | tf_op jit(solution)/shard_map/reshape | solution.py:198
  4.2 52.0 %shard_map.103 = f32[8,128]{1,0:T(8,128)} custom-call(s32[64]{0:T(128)} %owner_ref.1, s32[16,8]{1,0:T(8,128)} %copy.11.partners_ref, s32[64,12]{1,0:T(8,128)} %copy.12.blocks_ref, f32[64]{0:T(128)} %occ_ref.1, bf16[64,16,256]{2,1,0:T(8,128)(2,1)} %three_ref.1, f32[16,16]{1,0:T(8,128)} %metric_ref.1, s32[64,256]{1,0:T(8,128)} %domains_ref.1, ...), custom_call_target="tpu_custom_call" | custom-call | tf_op jit(solution)/shard_map/pallas_call | solution.py:201
  56.2 0.0 copy-start
  56.2 1.2 %slice.11 = f32[1,1]{1,0:T(1,128)} slice(f32[8,128]{1,0:T(8,128)} %shard_map.103), slice={[4:5], [0:1]} | slice | bytes 8 | tf_op jit(solution)/shard_map/slice | solution.py:224
  57.4 1.3 %slice.10 = f32[4,8]{1,0:T(4,128)} slice(f32[8,128]{1,0:T(8,128)} %shard_map.103), slice={[0:4], [4:12]} | slice | bytes 256 | tf_op jit(solution)/shard_map/slice | solution.py:224
  58.8 0.0 copy-done
  58.8 0.6 slice.9
Async XLA Ops:
  0.6 1.4 %copy-start.1 = (s32[64,12]{0,1:T(8,128)S(1)}, s32[64,12]{0,1:T(8,128)}, u32[]{:S(2)}) copy-start(s32[64,12]{0,1:T(8,128)} %param.10) | copy-start | bytes 9220
  56.2 2.6 %copy-start = (f32[8,128]{1,0:T(8,128)S(1)}, f32[8,128]{1,0:T(8,128)}, u32[]{:S(2)}) copy-start(f32[8,128]{1,0:T(8,128)} %shard_map.103) | copy-start | bytes 12292

commit v2 on v1

--- a/solution.py
+++ b/solution.py
@@ -14,9 +14,9 @@
 def kernel(
     n, slab, npart,
     owner_ref, partners_ref, blocks_ref, occ_ref,
-    three_ref, metric_ref, domains_ref, table_ref,
+    three_ref, metric_ref, domains_ref, virt_ref,
     out_ref,
-    fitted, send, recv, inverse, left_t, gaps, sums, totals,
+    fitted, send, recv, table_ref, inverse, left_t, gaps, sums, totals,
     send_sem, recv_sem, tot_send_sem, tot_recv_sem,
 ):
     me = lax.axis_index("aux")
@@ -29,7 +29,7 @@
         return lax.rem(me + 1 + lax.rem(step + order_start, n - 1), n)
 
     def orbital(t, slot):
-        return owner_ref[t * slab + slot] if slot < slab else partners_ref[t, slot - slab]
+        return owner_ref[t * slab + slot] if slot < slab else partners_ref[slot - slab, t]
 
     barrier = pltpu.get_barrier_semaphore()
 
@@ -90,6 +90,13 @@
         recv[me, slot] = fitted[orbital(me, slot)]
 
     depth = table_ref.shape[0]
+    n_virt = virt_ref.shape[0]
+    full = n_virt // LANES
+    table_ref[...] = jnp.zeros_like(table_ref)
+    for row in range(full):
+        table_ref[row, :] = virt_ref[pl.ds(row * LANES, LANES)]
+    if n_virt % LANES:
+        table_ref[full, 0 : n_virt % LANES] = virt_ref[pl.ds(full * LANES, n_virt % LANES)]
     by_lane = table_ref[...].T
     for slot in range(joined):
         one = orbital(me, slot)
@@ -122,10 +129,10 @@
         one = orbital(me, i)
 
         def hit(f, found, one=one):
-            return jnp.where(block_of == blocks_ref[one, f], 1.0, found)
+            return jnp.where(block_of == blocks_ref[f, one], 1.0, found)
 
         mask = lax.fori_loop(
-            0, blocks_ref.shape[1], hit, jnp.zeros((1, width_p), jnp.float32), unroll=width_p <= 512
+            0, blocks_ref.shape[0], hit, jnp.zeros((1, width_p), jnp.float32), unroll=width_p <= 512
         )
         turned = recv[:, i].reshape(width_p, width).astype(jnp.float32).T
         left_t[i] = (turned * mask).astype(jnp.bfloat16)
@@ -185,6 +192,13 @@
     lax.fori_loop(0, n - 1, finish, 0)
 
 
+def split_outputs(table_ref, slab_ref, partner_ref, total_ref):
+    slab, npart = partner_ref.shape
+    slab_ref[...] = table_ref[0:slab, 0:slab]
+    partner_ref[...] = table_ref[0:slab, slab : slab + npart]
+    total_ref[...] = table_ref[slab : slab + 1, 0:1]
+
+
 def per_device(
     three_index, fit_metric, fit_blocks, domains, occ_energy, virt_energy, owner_map, partners
 ):
@@ -194,8 +208,7 @@
     npart = partners.shape[1]
     joined = slab + npart
     chunk = 8 * LANES
-    length = -(-virt_energy.shape[0] // chunk) * chunk
-    table = jnp.pad(virt_energy, (0, length - virt_energy.shape[0])).reshape(-1, LANES)
+    depth = -(-virt_energy.shape[0] // chunk) * 8
     smem = pl.BlockSpec(memory_space=pltpu.SMEM)
     vmem = pl.BlockSpec(memory_space=pltpu.VMEM)
     out = pl.pallas_call(
@@ -207,6 +220,7 @@
             pltpu.VMEM((total_occ, rows, width), jnp.bfloat16),
             pltpu.VMEM((n, joined, rows, width), jnp.bfloat16),
             pltpu.VMEM((n, joined, rows, width), jnp.bfloat16),
+            pltpu.VMEM((depth, LANES), jnp.float32),
             pltpu.VMEM((slab, joined, width, width), jnp.float32),
             pltpu.VMEM((slab, width, n * rows), jnp.bfloat16),
             pltpu.VMEM((-(-joined // 8) * 8, width), jnp.float32),
@@ -220,8 +234,20 @@
         compiler_params=pltpu.CompilerParams(
             collective_id=0, has_side_effects=True, vmem_limit_bytes=56 * 1024 * 1024
         ),
-    )(owner_map, partners, fit_blocks, occ_energy, three_index, fit_metric, domains, table)
-    return out[:slab, :slab], out[:slab, slab:joined], out[slab, :1]
+    )(
+        owner_map, partners.T, fit_blocks.T, occ_energy, three_index, fit_metric, domains, virt_energy
+    )
+    slab_energy, partner_energy, total = pl.pallas_call(
+        split_outputs,
+        out_shape=(
+            jax.ShapeDtypeStruct((slab, slab), jnp.float32),
+            jax.ShapeDtypeStruct((slab, npart), jnp.float32),
+            jax.ShapeDtypeStruct((1, 1), jnp.float32),
+        ),
+        in_specs=[vmem],
+        out_specs=(vmem, vmem, vmem),
+    )(out)
+    return slab_energy, partner_energy, total.reshape(1)
 
 
 def solution(mesh):

time: 59.7 us -> 53.7 us (0.90)
  local copies, waits for them, and re-layouts: 6.72 us -> 0 us
  Pallas kernels: 52 us -> 52.9 us
    slice x3 -> x0, local copies, waits for them, and re-layouts: 3.14 us -> none  [per_device(): return (out[:slab, :slab], out[:slab, slab:joined], out[slab, :1])]
    unnamed x6 -> x0, local copies, waits for them, and re-layouts: 2.07 us -> none
    reshape x1 -> x0, local copies, waits for them, and re-layouts: 1.51 us -> none  [per_device(): jnp.pad(virt_energy, (0, length - virt_energy.shape[0])).reshape(-1, LANES)]
    pallas_call x0 -> x1, Pallas kernels: none -> 1.32 us  [per_device(): pl.pallas_call(split_outputs, out_shape=(jax.ShapeDtypeStruct((slab, slab...]
where the time goes in v2:
time: 53.7 us; the launch traced here: 53.5 us
  Pallas kernels  52.9 us (99%)
  between operations  0.64 us (1%)
    pallas_call x1, Pallas kernels, per_device(): pl.pallas_call(functools.partial(kernel, n, slab, npart), out_shape=jax.S...  51.6 us
    pallas_call x1, Pallas kernels, per_device(): pl.pallas_call(split_outputs, out_shape=(jax.ShapeDtypeStruct((slab, slab...  1.32 us

profile of v2, /device:TPU:0, one launch (start us, length us, event | category | flops | bytes accessed | tf_op | source)
XLA Modules:
  0.0 53.5 jit_solution(12228137504711676914)
XLA Ops:
  0.6 51.6 %shard_map.103.table_ref = f32[8,128]{1,0:T(8,128)} custom-call(s32[64]{0:T(128)} %owner_ref.1, s32[8,16]{1,0:T(8,128)} %bitcast.4, s32[12,64]{1,0:T(8,128)} %bitcast.3, f32[64]{0:T(128)} %occ_ref.1, bf16[64,16,256]{2,1,0:T(8,128)(2,1)} %three_ref.1, f32[16,16]{1,0:T(8,128)} %metric_ref.1, s32[64,256]{1,0:T(8,128)} %domains_ref.1, f32[20000]{0:T(1024)} %virt_ref.1), custom_call_target="tpu_custom_call" | custom-call | tf_op jit(solution)/shard_map/pallas_call | solution.py:214
  52.2 1.3 %shard_map.104 = (f32[4,4]{1,0:T(4,128)}, f32[4,8]{1,0:T(4,128)}, f32[1,1]{1,0:T(1,128)}) custom-call(f32[8,128]{1,0:T(8,128)} %shard_map.103.table_ref), custom_call_target="tpu_custom_call" | custom-call | tf_op jit(solution)/shard_map/pallas_call | solution.py:240

commit v3 on v2

--- a/solution.py
+++ b/solution.py
@@ -16,14 +16,23 @@
     owner_ref, partners_ref, blocks_ref, occ_ref,
     three_ref, metric_ref, domains_ref, virt_ref,
     out_ref,
-    fitted, send, recv, table_ref, inverse, left_t, gaps, sums, totals,
-    send_sem, recv_sem, tot_send_sem, tot_recv_sem,
+    fitted, cross_a, cross_b, send, relay, recv, table_ref, inverse, left_t, gaps, sums, totals,
+    cross_send_sem, cross_recv_sem, send_sem, relay_sem, recv_sem, tot_send_sem, tot_recv_sem,
 ):
     me = lax.axis_index("aux")
     total_occ, rows, width = three_ref.shape
     width_p = n * rows
     joined = slab + npart
-    order_start = max(n // 2 - 1, 0)
+    order_start = n // 2 - 1
+    half = n // 2
+    here = lax.rem(me, half)
+    base = me - here
+    across = lax.rem(me + half, n)
+    crossed = (cross_a, cross_b)
+    part = width // 2
+
+    def near(step):
+        return base + lax.rem(here + 1 + step, half)
 
     def peer(step):
         return lax.rem(me + 1 + lax.rem(step + order_start, n - 1), n)
@@ -64,30 +73,68 @@
         done = jnp.dot(third, block, preferred_element_type=jnp.float32)
         done += jnp.dot(second, block, preferred_element_type=jnp.float32)
         done += jnp.dot(first, block, preferred_element_type=jnp.float32)
-        fitted[pl.ds(g * group, group)] = done.astype(jnp.bfloat16).reshape(group, rows, width)
+        done = done.astype(jnp.bfloat16)
+        for c in range(2):
+            piece = done[:, c * part : (c + 1) * part].reshape(group, rows, part)
+            fitted[c, pl.ds(g * group, group)] = piece
         return carry
 
     lax.fori_loop(0, total_occ // group, fit, 0)
 
     pl.semaphore_wait(barrier, n - 1)
+
+    def cross_copy(c):
+        return pltpu.make_async_remote_copy(
+            src_ref=fitted.at[c], dst_ref=crossed[c],
+            send_sem=cross_send_sem.at[c], recv_sem=cross_recv_sem.at[c],
+            device_id={"aux": across}, device_id_type=pl.DeviceIdType.MESH,
+        )
+
+    for c in range(2):
+        cross_copy(c).start()
 
     def block_copy(target, source):
         return pltpu.make_async_remote_copy(
-            src_ref=send.at[target], dst_ref=recv.at[source],
-            send_sem=send_sem.at[target], recv_sem=recv_sem.at[source],
+            src_ref=send.at[lax.rem(target, half)], dst_ref=recv.at[source],
+            send_sem=send_sem.at[lax.rem(target, half)], recv_sem=recv_sem.at[2, source],
             device_id={"aux": target}, device_id_type=pl.DeviceIdType.MESH,
         )
 
+    def relay_copy(c, target, source):
+        return pltpu.make_async_remote_copy(
+            src_ref=relay.at[c, lax.rem(target, half)], dst_ref=recv.at[source, c],
+            send_sem=relay_sem.at[c, lax.rem(target, half)], recv_sem=recv_sem.at[c, source],
+            device_id={"aux": target}, device_id_type=pl.DeviceIdType.MESH,
+        )
+
     def pack(step, carry):
-        t = peer(step)
+        t = near(step)
         for slot in range(joined):
-            send[t, slot] = fitted[orbital(t, slot)]
+            one = orbital(t, slot)
+            for c in range(2):
+                send[lax.rem(t, half), c, slot] = fitted[c, one]
         block_copy(t, me).start()
         return carry
 
-    lax.fori_loop(0, n - 1, pack, 0)
+    lax.fori_loop(0, half - 1, pack, 0)
     for slot in range(joined):
-        recv[me, slot] = fitted[orbital(me, slot)]
+        one = orbital(me, slot)
+        for c in range(2):
+            recv[me, c, slot] = fitted[c, one]
+
+    def hand_on(c):
+        cross_copy(c).wait_recv()
+
+        def forward(step, carry):
+            t = near(step)
+            for slot in range(joined):
+                relay[c, lax.rem(t, half), slot] = crossed[c][orbital(t, slot)]
+            relay_copy(c, t, across).start()
+            return carry
+
+        lax.fori_loop(0, half - 1, forward, 0)
+        for slot in range(joined):
+            recv[across, c, slot] = crossed[c][orbital(me, slot)]
 
     depth = table_ref.shape[0]
     n_virt = virt_ref.shape[0]
@@ -107,6 +154,7 @@
         values = jnp.dot(by_lane, pick, precision=HIGHEST, preferred_element_type=jnp.float32)
         chosen = jnp.where(lax.broadcasted_iota(jnp.int32, (LANES, width), 0) == low, values, 0.0)
         gaps[pl.ds(slot, 1), :] = jnp.sum(chosen, axis=0, keepdims=True) - occ_ref[one]
+    hand_on(0)
     for i in range(slab):
         down = jnp.broadcast_to(gaps[pl.ds(i, 1), :], (width, width)).T
 
@@ -117,12 +165,21 @@
         lax.fori_loop(0, joined, invert, 0)
     sums[...] = jnp.zeros_like(sums)
 
+    hand_on(1)
+
     def arrive(step, carry):
-        source = peer(step)
-        block_copy(source, source).wait_recv()
-        return carry
-
-    lax.fori_loop(0, n - 1, arrive, 0)
+        t = near(step)
+        block_copy(t, t).wait_recv()
+        source = lax.rem(t + half, n)
+        for c in range(2):
+            relay_copy(c, t, source).wait_recv()
+        return carry
+
+    lax.fori_loop(0, half - 1, arrive, 0)
+
+    def whole_block(slot):
+        parts = [recv[:, c, slot].reshape(width_p, part) for c in range(2)]
+        return jnp.concatenate(parts, axis=1)
 
     block_of = lax.broadcasted_iota(jnp.int32, (1, width_p), 1) // rows
     for i in range(slab):
@@ -134,13 +191,13 @@
         mask = lax.fori_loop(
             0, blocks_ref.shape[0], hit, jnp.zeros((1, width_p), jnp.float32), unroll=width_p <= 512
         )
-        turned = recv[:, i].reshape(width_p, width).astype(jnp.float32).T
+        turned = whole_block(i).astype(jnp.float32).T
         left_t[i] = (turned * mask).astype(jnp.bfloat16)
 
     def pairs(i, carry):
         left = left_t[i]
         for j in range(joined):
-            right = recv[:, j].reshape(width_p, width)
+            right = whole_block(j)
             coulomb = jnp.dot(left, right, preferred_element_type=jnp.float32)
             terms = coulomb * coulomb * inverse[i, j]
             sums[i, pl.ds(j, 1), :] = jnp.sum(terms, axis=0, keepdims=True)
@@ -185,11 +242,21 @@
 
     def finish(step, carry):
         t = peer(step)
+        total_copy(t, me).wait_send()
+        return carry
+
+    lax.fori_loop(0, n - 1, finish, 0)
+
+    def finish_near(step, carry):
+        t = near(step)
         block_copy(t, me).wait_send()
-        total_copy(t, me).wait_send()
-        return carry
-
-    lax.fori_loop(0, n - 1, finish, 0)
+        for c in range(2):
+            relay_copy(c, t, across).wait_send()
+        return carry
+
+    lax.fori_loop(0, half - 1, finish_near, 0)
+    for c in range(2):
+        cross_copy(c).wait_send()
 
 
 def split_outputs(table_ref, slab_ref, partner_ref, total_ref):
@@ -217,17 +284,23 @@
         in_specs=[smem] * 4 + [vmem] * 4,
         out_specs=vmem,
         scratch_shapes=[
-            pltpu.VMEM((total_occ, rows, width), jnp.bfloat16),
-            pltpu.VMEM((n, joined, rows, width), jnp.bfloat16),
-            pltpu.VMEM((n, joined, rows, width), jnp.bfloat16),
+            pltpu.VMEM((2, total_occ, rows, width // 2), jnp.bfloat16),
+            pltpu.VMEM((total_occ, rows, width // 2), jnp.bfloat16),
+            pltpu.VMEM((total_occ, rows, width // 2), jnp.bfloat16),
+            pltpu.VMEM((n // 2, 2, joined, rows, width // 2), jnp.bfloat16),
+            pltpu.VMEM((2, n // 2, joined, rows, width // 2), jnp.bfloat16),
+            pltpu.VMEM((n, 2, joined, rows, width // 2), jnp.bfloat16),
             pltpu.VMEM((depth, LANES), jnp.float32),
             pltpu.VMEM((slab, joined, width, width), jnp.float32),
             pltpu.VMEM((slab, width, n * rows), jnp.bfloat16),
             pltpu.VMEM((-(-joined // 8) * 8, width), jnp.float32),
             pltpu.VMEM((slab, LANES, width), jnp.float32),
             pltpu.VMEM((n, 8, LANES), jnp.float32),
-            pltpu.SemaphoreType.DMA((n,)),
-            pltpu.SemaphoreType.DMA((n,)),
+            pltpu.SemaphoreType.DMA((2,)),
+            pltpu.SemaphoreType.DMA((2,)),
+            pltpu.SemaphoreType.DMA((n // 2,)),
+            pltpu.SemaphoreType.DMA((2, n // 2)),
+            pltpu.SemaphoreType.DMA((3, n)),
             pltpu.SemaphoreType.DMA((n,)),
             pltpu.SemaphoreType.DMA((n,)),
         ],

time: 53.7 us -> 49.6 us (0.924)
  Pallas kernels: 52.9 us -> 48.7 us
    pallas_call x1, Pallas kernels: 51.6 us -> 47.4 us  [per_device(): pl.pallas_call(functools.partial(kernel, n, slab, npart), out_shape=jax.S...]
where the time goes in v3:
time: 49.6 us; the launch traced here: 49.4 us
  Pallas kernels  48.7 us (98%)
  between operations  0.64 us (1%)
    pallas_call x1, Pallas kernels, per_device(): pl.pallas_call(functools.partial(kernel, n, slab, npart), out_shape=jax.S...  47.4 us
    pallas_call x1, Pallas kernels, per_device(): pl.pallas_call(split_outputs, out_shape=(jax.ShapeDtypeStruct((slab, slab...  1.32 us

profile of v3, /device:TPU:0, one launch (start us, length us, event | category | flops | bytes accessed | tf_op | source)
XLA Modules:
  0.0 49.4 jit_solution(1237620973421876908)
XLA Ops:
  0.6 47.4 %shard_map.103.table_ref = f32[8,128]{1,0:T(8,128)} custom-call(s32[64]{0:T(128)} %owner_ref.1, s32[8,16]{1,0:T(8,128)} %bitcast.4, s32[12,64]{1,0:T(8,128)} %bitcast.3, f32[64]{0:T(128)} %occ_ref.1, bf16[64,16,256]{2,1,0:T(8,128)(2,1)} %three_ref.1, f32[16,16]{1,0:T(8,128)} %metric_ref.1, s32[64,256]{1,0:T(8,128)} %domains_ref.1, f32[20000]{0:T(1024)} %virt_ref.1), custom_call_target="tpu_custom_call" | custom-call | tf_op jit(solution)/shard_map/pallas_call | solution.py:281
  48.1 1.3 %shard_map.104 = (f32[4,4]{1,0:T(4,128)}, f32[4,8]{1,0:T(4,128)}, f32[1,1]{1,0:T(1,128)}) custom-call(f32[8,128]{1,0:T(8,128)} %shard_map.103.table_ref), custom_call_target="tpu_custom_call" | custom-call | tf_op jit(solution)/shard_map/pallas_call | solution.py:313

commit v4 on v3

--- a/solution.py
+++ b/solution.py
@@ -16,7 +16,7 @@
     owner_ref, partners_ref, blocks_ref, occ_ref,
     three_ref, metric_ref, domains_ref, virt_ref,
     out_ref,
-    fitted, cross_a, cross_b, send, relay, recv, table_ref, inverse, left_t, gaps, sums, totals,
+    fitted_a, fitted_b, cross_a, cross_b, send, relay, recv, table_ref, inverse, left_t, gaps, masks, sums, totals,
     cross_send_sem, cross_recv_sem, send_sem, relay_sem, recv_sem, tot_send_sem, tot_recv_sem,
 ):
     me = lax.axis_index("aux")
@@ -29,6 +29,7 @@
     base = me - here
     across = lax.rem(me + half, n)
     crossed = (cross_a, cross_b)
+    fitted = (fitted_a, fitted_b)
     part = width // 2
 
     def near(step):
@@ -68,30 +69,29 @@
     second = rest.astype(jnp.bfloat16)
     third = (rest - second.astype(jnp.float32)).astype(jnp.bfloat16)
 
-    def fit(g, carry):
-        block = three_ref[pl.ds(g * group, group)].reshape(side, width)
-        done = jnp.dot(third, block, preferred_element_type=jnp.float32)
-        done += jnp.dot(second, block, preferred_element_type=jnp.float32)
-        done += jnp.dot(first, block, preferred_element_type=jnp.float32)
-        done = done.astype(jnp.bfloat16)
-        for c in range(2):
-            piece = done[:, c * part : (c + 1) * part].reshape(group, rows, part)
-            fitted[c, pl.ds(g * group, group)] = piece
-        return carry
-
-    lax.fori_loop(0, total_occ // group, fit, 0)
-
+    def fit_half(c):
+        def fit(g, carry):
+            block = three_ref[pl.ds(g * group, group), :, c * part : (c + 1) * part].reshape(side, part)
+            done = jnp.dot(third, block, preferred_element_type=jnp.float32)
+            done += jnp.dot(second, block, preferred_element_type=jnp.float32)
+            done += jnp.dot(first, block, preferred_element_type=jnp.float32)
+            fitted[c][pl.ds(g * group, group)] = done.astype(jnp.bfloat16).reshape(group, rows, part)
+            return carry
+
+        lax.fori_loop(0, total_occ // group, fit, 0)
+
+    fit_half(0)
     pl.semaphore_wait(barrier, n - 1)
 
     def cross_copy(c):
         return pltpu.make_async_remote_copy(
-            src_ref=fitted.at[c], dst_ref=crossed[c],
+            src_ref=fitted[c], dst_ref=crossed[c],
             send_sem=cross_send_sem.at[c], recv_sem=cross_recv_sem.at[c],
             device_id={"aux": across}, device_id_type=pl.DeviceIdType.MESH,
         )
 
-    for c in range(2):
-        cross_copy(c).start()
+    cross_copy(0).start()
+    fit_half(1)
 
     def block_copy(target, source):
         return pltpu.make_async_remote_copy(
@@ -112,7 +112,7 @@
         for slot in range(joined):
             one = orbital(t, slot)
             for c in range(2):
-                send[lax.rem(t, half), c, slot] = fitted[c, one]
+                send[lax.rem(t, half), c, slot] = fitted[c][one]
         block_copy(t, me).start()
         return carry
 
@@ -120,7 +120,7 @@
     for slot in range(joined):
         one = orbital(me, slot)
         for c in range(2):
-            recv[me, c, slot] = fitted[c, one]
+            recv[me, c, slot] = fitted[c][one]
 
     def hand_on(c):
         cross_copy(c).wait_recv()
@@ -154,6 +154,8 @@
         values = jnp.dot(by_lane, pick, precision=HIGHEST, preferred_element_type=jnp.float32)
         chosen = jnp.where(lax.broadcasted_iota(jnp.int32, (LANES, width), 0) == low, values, 0.0)
         gaps[pl.ds(slot, 1), :] = jnp.sum(chosen, axis=0, keepdims=True) - occ_ref[one]
+    cross_copy(0).wait_send()
+    cross_copy(1).start()
     hand_on(0)
     for i in range(slab):
         down = jnp.broadcast_to(gaps[pl.ds(i, 1), :], (width, width)).T
@@ -165,34 +167,45 @@
         lax.fori_loop(0, joined, invert, 0)
     sums[...] = jnp.zeros_like(sums)
 
-    hand_on(1)
-
-    def arrive(step, carry):
+    block_of = lax.broadcasted_iota(jnp.int32, (1, width_p), 1) // rows
+    for i in range(slab):
+        one = orbital(me, i)
+
+        def hit(f, found, one=one):
+            return jnp.where(block_of == blocks_ref[f, one], 1.0, found)
+
+        masks[pl.ds(i, 1), :] = lax.fori_loop(
+            0, blocks_ref.shape[0], hit, jnp.zeros((1, width_p), jnp.float32), unroll=width_p <= 512
+        )
+
+    def turn(c):
+        for i in range(slab):
+            turned = recv[:, c, i].reshape(width_p, part).astype(jnp.float32).T
+            left_t[i, c * part : (c + 1) * part] = (turned * masks[pl.ds(i, 1), :]).astype(jnp.bfloat16)
+
+    def arrive_near(step, carry):
         t = near(step)
         block_copy(t, t).wait_recv()
-        source = lax.rem(t + half, n)
-        for c in range(2):
-            relay_copy(c, t, source).wait_recv()
-        return carry
-
-    lax.fori_loop(0, half - 1, arrive, 0)
+        return carry
+
+    def arrive(c):
+        def one_source(step, carry):
+            t = near(step)
+            relay_copy(c, t, lax.rem(t + half, n)).wait_recv()
+            return carry
+
+        lax.fori_loop(0, half - 1, one_source, 0)
+
+    hand_on(1)
+    lax.fori_loop(0, half - 1, arrive_near, 0)
+    arrive(0)
+    turn(0)
+    arrive(1)
+    turn(1)
 
     def whole_block(slot):
         parts = [recv[:, c, slot].reshape(width_p, part) for c in range(2)]
         return jnp.concatenate(parts, axis=1)
-
-    block_of = lax.broadcasted_iota(jnp.int32, (1, width_p), 1) // rows
-    for i in range(slab):
-        one = orbital(me, i)
-
-        def hit(f, found, one=one):
-            return jnp.where(block_of == blocks_ref[f, one], 1.0, found)
-
-        mask = lax.fori_loop(
-            0, blocks_ref.shape[0], hit, jnp.zeros((1, width_p), jnp.float32), unroll=width_p <= 512
-        )
-        turned = whole_block(i).astype(jnp.float32).T
-        left_t[i] = (turned * mask).astype(jnp.bfloat16)
 
     def pairs(i, carry):
         left = left_t[i]
@@ -255,8 +268,7 @@
         return carry
 
     lax.fori_loop(0, half - 1, finish_near, 0)
-    for c in range(2):
-        cross_copy(c).wait_send()
+    cross_copy(1).wait_send()
 
 
 def split_outputs(table_ref, slab_ref, partner_ref, total_ref):
@@ -284,7 +296,8 @@
         in_specs=[smem] * 4 + [vmem] * 4,
         out_specs=vmem,
         scratch_shapes=[
-            pltpu.VMEM((2, total_occ, rows, width // 2), jnp.bfloat16),
+            pltpu.VMEM((total_occ, rows, width // 2), jnp.bfloat16),
+            pltpu.VMEM((total_occ, rows, width // 2), jnp.bfloat16),
             pltpu.VMEM((total_occ, rows, width // 2), jnp.bfloat16),
             pltpu.VMEM((total_occ, rows, width // 2), jnp.bfloat16),
             pltpu.VMEM((n // 2, 2, joined, rows, width // 2), jnp.bfloat16),
@@ -294,6 +307,7 @@
             pltpu.VMEM((slab, joined, width, width), jnp.float32),
             pltpu.VMEM((slab, width, n * rows), jnp.bfloat16),
             pltpu.VMEM((-(-joined // 8) * 8, width), jnp.float32),
+            pltpu.VMEM((8, n * rows), jnp.float32),
             pltpu.VMEM((slab, LANES, width), jnp.float32),
             pltpu.VMEM((n, 8, LANES), jnp.float32),
             pltpu.SemaphoreType.DMA((2,)),

time: 49.6 us -> 48.8 us (0.984)
  Pallas kernels: 48.7 us -> 48 us
    pallas_call x1, Pallas kernels: 47.4 us -> 46.6 us  [per_device(): pl.pallas_call(functools.partial(kernel, n, slab, npart), out_shape=jax.S...]
where the time goes in v4:
time: 48.8 us; the launch traced here: 48.6 us
  Pallas kernels  48 us (98%)
  between operations  0.64 us (1%)
    pallas_call x1, Pallas kernels, per_device(): pl.pallas_call(functools.partial(kernel, n, slab, npart), out_shape=jax.S...  46.6 us
    pallas_call x1, Pallas kernels, per_device(): pl.pallas_call(split_outputs, out_shape=(jax.ShapeDtypeStruct((slab, slab...  1.32 us

profile of v4, /device:TPU:0, one launch (start us, length us, event | category | flops | bytes accessed | tf_op | source)
XLA Modules:
  0.0 48.6 jit_solution(4714384122602065336)
XLA Ops:
  0.6 46.6 %shard_map.103.table_ref = f32[8,128]{1,0:T(8,128)} custom-call(s32[64]{0:T(128)} %owner_ref.1, s32[8,16]{1,0:T(8,128)} %bitcast.4, s32[12,64]{1,0:T(8,128)} %bitcast.3, f32[64]{0:T(128)} %occ_ref.1, bf16[64,16,256]{2,1,0:T(8,128)(2,1)} %three_ref.1, f32[16,16]{1,0:T(8,128)} %metric_ref.1, s32[64,256]{1,0:T(8,128)} %domains_ref.1, f32[20000]{0:T(1024)} %virt_ref.1), custom_call_target="tpu_custom_call" | custom-call | tf_op jit(solution)/shard_map/pallas_call | solution.py:293
  47.3 1.3 %shard_map.104 = (f32[4,4]{1,0:T(4,128)}, f32[4,8]{1,0:T(4,128)}, f32[1,1]{1,0:T(1,128)}) custom-call(f32[8,128]{1,0:T(8,128)} %shard_map.103.table_ref), custom_call_target="tpu_custom_call" | custom-call | tf_op jit(solution)/shard_map/pallas_call | solution.py:327

commit v5 on v4

--- a/solution.py
+++ b/solution.py
@@ -25,6 +25,7 @@
     joined = slab + npart
     order_start = n // 2 - 1
     half = n // 2
+    quarter = half // 2
     here = lax.rem(me, half)
     base = me - here
     across = lax.rem(me + half, n)
@@ -33,7 +34,9 @@
     part = width // 2
 
     def near(step):
-        return base + lax.rem(here + 1 + step, half)
+        turn_over = lax.div(step, quarter)
+        layer = lax.rem(lax.div(here, quarter) + 1 + turn_over, 2)
+        return base + layer * quarter + lax.rem(here + step + turn_over, quarter)
 
     def peer(step):
         return lax.rem(me + 1 + lax.rem(step + order_start, n - 1), n)

time: 48.8 us -> 48.8 us (level)
  no operation moved by 1% of the time
where the time goes in v5:
time: 48.8 us; the launch traced here: 48.6 us
  Pallas kernels  48 us (98%)
  between operations  0.64 us (1%)
    pallas_call x1, Pallas kernels, per_device(): pl.pallas_call(functools.partial(kernel, n, slab, npart), out_shape=jax.S...  46.7 us
    pallas_call x1, Pallas kernels, per_device(): pl.pallas_call(split_outputs, out_shape=(jax.ShapeDtypeStruct((slab, slab...  1.32 us

profile of v5, /device:TPU:0, one launch (start us, length us, event | category | flops | bytes accessed | tf_op | source)
XLA Modules:
  0.0 48.6 jit_solution(3355168677165157212)
XLA Ops:
  0.6 46.7 %shard_map.103.table_ref = f32[8,128]{1,0:T(8,128)} custom-call(s32[64]{0:T(128)} %owner_ref.1, s32[8,16]{1,0:T(8,128)} %bitcast.4, s32[12,64]{1,0:T(8,128)} %bitcast.3, f32[64]{0:T(128)} %occ_ref.1, bf16[64,16,256]{2,1,0:T(8,128)(2,1)} %three_ref.1, f32[16,16]{1,0:T(8,128)} %metric_ref.1, s32[64,256]{1,0:T(8,128)} %domains_ref.1, f32[20000]{0:T(1024)} %virt_ref.1), custom_call_target="tpu_custom_call" | custom-call | tf_op jit(solution)/shard_map/pallas_call | solution.py:296
  47.3 1.3 %shard_map.104 = (f32[4,4]{1,0:T(4,128)}, f32[4,8]{1,0:T(4,128)}, f32[1,1]{1,0:T(1,128)}) custom-call(f32[8,128]{1,0:T(8,128)} %shard_map.103.table_ref), custom_call_target="tpu_custom_call" | custom-call | tf_op jit(solution)/shard_map/pallas_call | solution.py:330
